TPU v7x, 256 devices: a whole 4x4x8 slice. The times are simulated.
256 devices in a mesh: row: 32 (over x, y, core), col: 8 (over z).
Axes of the slice: x: 4, y: 4, z: 8, core: 2. Of those that a mesh axis runs over, the one named last changes fastest.
Arguments:
- features: bfloat16 [262144, 128], P(('row', 'col')), may hold values from -6 to 6
- adjacency: bfloat16 [32, 8, 64, 256, 256], P('row', 'col'), as said below
- block_rows: int32 [32, 8, 64], P('row', 'col'), may hold values from 0 to 31
- block_cols: int32 [32, 8, 64], P('row', 'col'), may hold values from 0 to 127
- live_counts: int32 [32, 8], P('row', 'col'), may hold values from 8 to 64, as said below
- self_weight: bfloat16 [128, 256], replicated, may hold values from -0.5 to 0.5
- neigh_weight: bfloat16 [128, 256], replicated, may hold values from -4 to 4
- out_bias: float32 [256], replicated, may hold values from -3 to 3
Outputs:
- hidden_out: bfloat16 [262144, 256], P(('row', 'col'))
Inputs may be any that keep to these rules, and one draw needn't show every extreme that they name: `live_counts`: every tile has between 8 and 64 live slots; some tile has exactly 64 and some tile exactly 8. Slots at or past the count hold arbitrary blocks and indices. `adjacency`: entries are zero or positive.
All inputs are finite; a program needn't handle non-finite values.
Results may differ from a plain program's by a relative error of at most 0.0033.
Values may be sent and summed in bfloat16 or wider, within the bound.
A program may use at most 128 MiB of HBM per device.

v0:
```python
import jax
import jax.numpy as jnp
from jax import lax
from jax.sharding import PartitionSpec as P


def per_device(
    features, adjacency, block_rows, block_cols, live_counts, self_weight, neigh_weight, out_bias
):
    rows_dev, feat = features.shape
    block = adjacency.shape[-1]
    slots = adjacency.shape[2]
    ncols = lax.axis_size("col")
    nrows = lax.axis_size("row")
    row_blocks = ncols * rows_dev // block
    col_blocks = nrows * rows_dev // block
    tile = adjacency[0, 0]
    rows_here = block_rows[0, 0]
    cols_here = block_cols[0, 0]
    count = live_counts[0, 0]
    column_x = lax.all_gather(features, "row", axis=0, tiled=True)
    picked = column_x.reshape(col_blocks, block, feat)[cols_here]
    products = jnp.einsum("sij,sjf->sif", tile, picked, preferred_element_type=jnp.float32)
    valid = jnp.arange(slots) < count
    target = jnp.where(valid, rows_here, row_blocks)
    partial_value = (
        jnp.zeros((row_blocks + 1, block, feat), jnp.float32).at[target].add(products)[:row_blocks]
    )
    partial_value = partial_value.reshape(row_blocks * block, feat)
    row_weight = jnp.sum(tile, axis=-1, dtype=jnp.float32)
    weights = (
        jnp.zeros((row_blocks + 1, block), jnp.float32).at[target].add(row_weight)[:row_blocks]
    )
    weights = weights.reshape(row_blocks * block)
    summed, degree = lax.psum((partial_value, weights), "col")
    neigh_mean = (summed / (1.0 + degree)[:, None]).astype(jnp.bfloat16)
    own_rows = lax.all_gather(features, "col", axis=0, tiled=True)
    width = self_weight.shape[1] // ncols
    offset = lax.axis_index("col") * width
    self_part = lax.dynamic_slice_in_dim(self_weight, offset, width, 1)
    neigh_part = lax.dynamic_slice_in_dim(neigh_weight, offset, width, 1)
    bias_part = lax.dynamic_slice_in_dim(out_bias, offset, width, 0)
    total = jnp.dot(own_rows, self_part, preferred_element_type=jnp.float32)
    total = total + jnp.dot(neigh_mean, neigh_part, preferred_element_type=jnp.float32) + bias_part
    unit_slice = jax.nn.relu(total).astype(jnp.bfloat16)
    return lax.all_to_all(unit_slice, "col", split_axis=0, concat_axis=1, tiled=True)


def solution(mesh):
    in_specs = (
        P(("row", "col"), None),
        P("row", "col", None, None, None),
        P("row", "col", None),
        P("row", "col", None),
        P("row", "col"),
        P(),
        P(),
        P(),
    )
    out_specs = P(("row", "col"), None)
    return jax.shard_map(
        per_device, mesh=mesh, in_specs=in_specs, out_specs=out_specs, check_vma=False
    )
```

profile of v0, /device:TPU:1, one launch (start us, length us, event | category | flops | bytes accessed | tf_op | source)
XLA Modules:
  0.0 264.6 jit_solution(5626680710285014634)
XLA Ops:
  6.5 0.7 all-gather.5.cloned.1.call-update
  7.3 0.0 all-gather.3.cloned.1.call-start
  7.3 0.7 all-gather.3.cloned.1.call-update
  8.0 0.0 all-reduce.2.cloned.1.call-start
  8.7 0.7 fusion.12
  9.4 0.7 fusion.13
  10.0 62.1 %all-gather.5.cloned.1.call-done = bf16[32768,128]{1,0:T(8,128)(2,1)} async-done(((bf16[1024,128]{1,0:T(8,128)(2,1)}), bf16[32768,128]{1,0:T(8,128)(2,1)}) %all-gather.5.cloned.1.call-update) | async-done | bytes 8388624 | tf_op jit(solution)/shard_map/all_gather | solution.py:21
  72.1 6.4 %gather_fusion = bf16[64,256,128]{2,1,0:T(8,128)(2,1)} fusion(bf16[128,256,128]{2,1,0:T(8,128)(2,1)} %bitcast.37, s32[1024]{0:T(1024)S(1)} %pad_clamp_fusion), kind=kCustom, calls=%fused_computation | custom fusion | bytes 8388864 | tf_op jit(solution)/shard_map/gather | solution.py:22
  78.5 10.8 %fusion.5 = f32[64,256,128]{1,2,0:T(8,128)} fusion(bf16[64,256,128]{2,1,0:T(8,128)(2,1)} %gather_fusion, bf16[1,1,64,256,256]{4,3,2,1,0:T(8,128)(2,1)} %param.9), kind=kOutput, calls=%fused_computation.12 | convolution fusion | flops 1073741824 | bytes 20971520 | tf_op jit(solution)/shard_map/sij,sjf->sif/dot_general | solution.py:23
  89.2 9.0 %copy.12 = f32[64,256,128]{2,1,0:T(8,128)} copy(f32[64,256,128]{1,2,0:T(8,128)} %fusion.5) | data formatting | bytes 16777216 | tf_op jit(solution)/shard_map/sij,sjf->sif/dot_general | solution.py:23
  98.2 2.5 broadcast_in_dim.8
  100.7 19.8 %scatter_fusion = f32[33,256,128]{2,1,0:T(8,128)} fusion(f32[33,256,128]{2,1,0:T(8,128)} %broadcast_in_dim.8, s32[64]{0:T(128)S(1)} %fusion.13, f32[64,256,128]{2,1,0:T(8,128)} %copy.12), kind=kCustom, calls=%fused_computation.1 | custom fusion | flops 2097152 | bytes 25166080 | tf_op jit(solution)/shard_map/scatter-add | solution.py:27
  120.6 4.6 %slice.10 = f32[32,256,128]{2,1,0:T(8,128)} slice(f32[33,256,128]{2,1,0:T(8,128)} %scatter_fusion), slice={[0:32], [0:256], [0:128]} | slice | bytes 8388608 | tf_op jit(solution)/shard_map/slice | solution.py:27
  125.1 0.0 all-reduce.2.cloned.1.call-update
  125.2 5.6 %convert_reduce_fusion = f32[64,256]{1,0:T(8,128)S(1)} fusion(bf16[1,1,64,256,256]{4,3,2,1,0:T(8,128)(2,1)} %param.9), kind=kLoop, calls=%fused_computation.3 | loop fusion | flops 8372224 | bytes 8454144 | tf_op jit(solution)/shard_map/reduce_sum | solution.py:30
  130.8 1.0 scatter_custom_fusion.1
  131.9 0.1 dynamic_slice.11
  131.9 26.7 %psum.15 = f32[8192]{0:T(1024)S(1)} all-reduce(f32[8192]{0:T(1024)S(1)} %bitcast.41), channel_id=1, replica_groups=mesh['row'=32,'col'=8] {'col'}, use_global_device_ids=true, to_apply=%region_4.5 | all-reduce | flops 8192 | bytes 65536 | tf_op jit(solution)/shard_map/psum | solution.py:35
  158.7 0.0 all-gather.3.cloned.1.call-done
  158.7 2.5 convolution_bitcast_fusion
  161.2 72.5 %all-reduce.2.cloned.1.call-done = f32[8192,128]{1,0:T(8,128)} async-done(((f32[8192,128]{1,0:T(8,128)}), f32[8192,128]{1,0:T(8,128)}) %all-reduce.2.cloned.1.call-update) | async-done | bytes 4194320 | tf_op jit(solution)/shard_map/psum | solution.py:35
  233.8 3.3 %fusion.2 = bf16[8192,32]{0,1:T(8,128)(2,1)S(1)} fusion(f32[8192,32]{0,1:T(8,128)S(1)} %convolution_bitcast_fusion, f32[8192,128]{1,0:T(8,128)} %all-reduce.2.cloned.1.call-done, f32[8192]{0:T(1024)S(1)} %broadcast_add_fusion, f32[32]{0:T(128)S(1)} %dynamic_slice.11, bf16[128,256]{1,0:T(8,128)(2,1)S(1)} %copy-done.1, s32[]{:T(128)S(6)} %select_n.37), kind=kOutput, calls=%fused_computation.8 | convolution fusion | flops 70254592 | bytes 5833220 | tf_op jit(solution)/shard_map/dot_general | solution.py:44
  237.1 19.9 %all_to_all.19 = bf16[8,1024,32]{1,2,0:T(8,128)(2,1)S(1)} all-to-all(bf16[8,1024,32]{1,2,0:T(8,128)(2,1)S(1)} %bitcast.38), channel_id=1, replica_groups=mesh['row'=32,'col'=8] {'col'}, dimensions={0} | all-to-all | bytes 1048576 | tf_op jit(solution)/shard_map/all_to_all | solution.py:46
  257.0 1.0 copy.14
  (12 shorter events, 0.1 us)
Async XLA Ops:
  6.5 152.2 %copy-start = (bf16[128,256]{1,0:T(8,128)(2,1)S(1)}, bf16[128,256]{1,0:T(8,128)(2,1)}, u32[]{:S(2)}) copy-start(bf16[128,256]{1,0:T(8,128)(2,1)} %param.13) | copy-start | bytes 196612
  6.5 65.5 %all-gather.5.cloned.1.call-start = ((), (), s32[]{:S(2)}) async-start(), calls=%async_computation.2 | async-start | bytes 8650752 | tf_op jit(solution)/shard_map/all_gather | solution.py:21
  7.3 151.4 %all-gather.3.cloned.1.call-start = ((), (), s32[]{:S(2)}) async-start(), calls=%async_computation.1 | async-start | bytes 2359296 | tf_op jit(solution)/shard_map/all_gather | solution.py:37
  8.0 225.7 %all-reduce.2.cloned.1.call-start = ((), (), s32[]{:S(2)}) async-start(), calls=%async_computation.3 | async-start | bytes 8388608 | tf_op jit(solution)/shard_map/psum | solution.py:35
  125.1 6.7 %copy-start.2 = (f32[256]{0:T(256)S(1)}, f32[256]{0:T(256)}, u32[]{:S(2)}) copy-start(f32[256]{0:T(256)} %param.15) | copy-start | bytes 3076
  125.2 108.6 %copy-start.1 = (bf16[128,256]{1,0:T(8,128)(2,1)S(1)}, bf16[128,256]{1,0:T(8,128)(2,1)}, u32[]{:S(2)}) copy-start(bf16[128,256]{1,0:T(8,128)(2,1)} %param.14) | copy-start | bytes 196612
Sparse Core Ops, SparseCore 0:
  9.9 62.1 all-gather.4
  73.9 36.6 all-gather.2
  125.3 108.4 all-reduce.1
where the time goes:
time: 266 us; the launch traced here: 265 us
  waiting for transfers between devices  136 us (51%)
  blocking collectives  46.7 us (18%)
  other arithmetic  27.8 us (10%)
  local copies, waits for them, and re-layouts  23.6 us (9%)
  matrix products  16.6 us (6%)
  between operations  13.9 us (5%)
    psum x1, waiting for transfers between devices, per_device(): summed, degree = lax.psum((partial_value, weights), 'col')  72.5 us
    all_gather x1, waiting for transfers between devices, per_device(): column_x = lax.all_gather(features, 'row', axis=0, tiled=True)  62.1 us
    psum x1, blocking collectives, per_device(): summed, degree = lax.psum((partial_value, weights), 'col')  26.7 us
    all_to_all x1, blocking collectives, per_device(): lax.all_to_all(unit_slice, 'col', split_axis=0, concat_axis=1, tiled=True)  19.9 us
    scatter-add x1, other arithmetic, per_device(): jnp.zeros((row_blocks + 1, block, feat), jnp.float32).at[target]  19.8 us
    dot_general x1, matrix products, per_device(): jnp.einsum('sij,sjf->sif', tile, picked, preferred_element_type=jnp.float32)  10.8 us
    dot_general x1, local copies, waits for them, and re-layouts, per_device(): jnp.einsum('sij,sjf->sif', tile, picked, preferred_element_type=jnp.float32)  9.01 us
    gather x1, local copies, waits for them, and re-layouts, per_device(): picked = column_x.reshape(col_blocks, block, feat)[cols_here]  6.39 us
  transfers between devices with their start and end apart: 3, of which 2 were waited for; matrix products, arithmetic and copies ran while one was open for 24% of the time, Pallas kernels for 0%

commit v1 on v0

--- a/solution.py
+++ b/solution.py
@@ -32,18 +32,12 @@
         jnp.zeros((row_blocks + 1, block), jnp.float32).at[target].add(row_weight)[:row_blocks]
     )
     weights = weights.reshape(row_blocks * block)
-    summed, degree = lax.psum((partial_value, weights), "col")
+    summed = lax.psum_scatter(partial_value, "col", scatter_dimension=0, tiled=True)
+    degree = lax.psum_scatter(weights, "col", scatter_dimension=0, tiled=True)
     neigh_mean = (summed / (1.0 + degree)[:, None]).astype(jnp.bfloat16)
-    own_rows = lax.all_gather(features, "col", axis=0, tiled=True)
-    width = self_weight.shape[1] // ncols
-    offset = lax.axis_index("col") * width
-    self_part = lax.dynamic_slice_in_dim(self_weight, offset, width, 1)
-    neigh_part = lax.dynamic_slice_in_dim(neigh_weight, offset, width, 1)
-    bias_part = lax.dynamic_slice_in_dim(out_bias, offset, width, 0)
-    total = jnp.dot(own_rows, self_part, preferred_element_type=jnp.float32)
-    total = total + jnp.dot(neigh_mean, neigh_part, preferred_element_type=jnp.float32) + bias_part
-    unit_slice = jax.nn.relu(total).astype(jnp.bfloat16)
-    return lax.all_to_all(unit_slice, "col", split_axis=0, concat_axis=1, tiled=True)
+    total = jnp.dot(features, self_weight, preferred_element_type=jnp.float32)
+    total = total + jnp.dot(neigh_mean, neigh_weight, preferred_element_type=jnp.float32) + out_bias
+    return jax.nn.relu(total).astype(jnp.bfloat16)
 
 
 def solution(mesh):

time: 266 us -> 190 us (0.71)
  waiting for transfers between devices: 136 us -> 83.6 us
  blocking collectives: 46.7 us -> 27 us
  matrix products: 16.6 us -> 13.2 us
    psum x1 -> x0, waiting for transfers between devices: 72.5 us -> none  [per_device(): summed, degree = lax.psum((partial_value, weights), 'col')]
    unnamed x0 -> x1, blocking collectives: none -> 27 us
    psum x1 -> x0, blocking collectives: 26.7 us -> none  [per_device(): summed, degree = lax.psum((partial_value, weights), 'col')]
    reduce_scatter x0 -> x1, waiting for transfers between devices: none -> 20 us  [per_device(): lax.psum_scatter(partial_value, 'col', scatter_dimension=0, tiled=True)]
    all_to_all x1 -> x0, blocking collectives: 19.9 us -> none  [per_device(): lax.all_to_all(unit_slice, 'col', split_axis=0, concat_axis=1, tiled=True)]
    dot_general x2, matrix products: 5.81 us -> 2.48 us  [the longest x1 2.21 us: per_device(): jnp.dot(neigh_mean, neigh_weight, preferred_element_type=jnp.float32)]
  transfers between devices with their start and end apart: 3 -> 2, of which waited for: 2 -> 2; matrix products, arithmetic and copies ran while one was open for 24% -> 5% of each run, Pallas kernels for 0% -> 0%
where the time goes in v1:
time: 190 us; the launch traced here: 189 us
  waiting for transfers between devices  83.6 us (44%)
  other arithmetic  27.8 us (15%)
  blocking collectives  27 us (14%)
  local copies, waits for them, and re-layouts  23.1 us (12%)
  between operations  14.8 us (8%)
  matrix products  13.2 us (7%)
    all_gather x1, waiting for transfers between devices, per_device(): column_x = lax.all_gather(features, 'row', axis=0, tiled=True)  62.8 us
    unnamed x1, blocking collectives  27 us
    reduce_scatter x1, waiting for transfers between devices, per_device(): lax.psum_scatter(partial_value, 'col', scatter_dimension=0, tiled=True)  20 us
    scatter-add x1, other arithmetic, per_device(): jnp.zeros((row_blocks + 1, block, feat), jnp.float32).at[target]  19.8 us
    dot_general x1, matrix products, per_device(): jnp.einsum('sij,sjf->sif', tile, picked, preferred_element_type=jnp.float32)  10.8 us
    dot_general x1, local copies, waits for them, and re-layouts, per_device(): jnp.einsum('sij,sjf->sif', tile, picked, preferred_element_type=jnp.float32)  8.99 us
    gather x1, local copies, waits for them, and re-layouts, per_device(): picked = column_x.reshape(col_blocks, block, feat)[cols_here]  6.39 us
    reduce_sum x1, other arithmetic, per_device(): row_weight = jnp.sum(tile, axis=-1, dtype=jnp.float32)  5.66 us
  transfers between devices with their start and end apart: 2, of which 2 were waited for; matrix products, arithmetic and copies ran while one was open for 5% of the time, Pallas kernels for 0%

profile of v1, /device:TPU:1, one launch (start us, length us, event | category | flops | bytes accessed | tf_op | source)
XLA Modules:
  0.0 189.4 jit_solution(13266795421112038594)
XLA Ops:
  6.5 0.0 copy-start
  6.5 0.0 all-gather.2.cloned.1.call-start
  6.5 0.7 all-gather.2.cloned.1.call-update
  7.3 0.0 reduce-scatter.2.cloned.1.call-start
  8.0 0.7 fusion.11
  8.6 0.7 fusion.12
  9.3 62.8 %all-gather.2.cloned.1.call-done = bf16[32768,128]{1,0:T(8,128)(2,1)} async-done(((bf16[1024,128]{1,0:T(8,128)(2,1)}), bf16[32768,128]{1,0:T(8,128)(2,1)}) %all-gather.2.cloned.1.call-update) | async-done | bytes 8388624 | tf_op jit(solution)/shard_map/all_gather | solution.py:21
  72.1 6.4 %gather_fusion = bf16[64,256,128]{2,1,0:T(8,128)(2,1)} fusion(bf16[128,256,128]{2,1,0:T(8,128)(2,1)} %bitcast.31, s32[1024]{0:T(1024)S(1)} %pad_clamp_fusion), kind=kCustom, calls=%fused_computation | custom fusion | bytes 8388864 | tf_op jit(solution)/shard_map/gather | solution.py:22
  78.5 10.8 %fusion.2 = f32[64,256,128]{1,2,0:T(8,128)} fusion(bf16[64,256,128]{2,1,0:T(8,128)(2,1)} %gather_fusion, bf16[1,1,64,256,256]{4,3,2,1,0:T(8,128)(2,1)} %param.9), kind=kOutput, calls=%fused_computation.6 | convolution fusion | flops 1073741824 | bytes 20971520 | tf_op jit(solution)/shard_map/sij,sjf->sif/dot_general | solution.py:23
  89.2 9.0 %copy.13 = f32[64,256,128]{2,1,0:T(8,128)} copy(f32[64,256,128]{1,2,0:T(8,128)} %fusion.2) | data formatting | bytes 16777216 | tf_op jit(solution)/shard_map/sij,sjf->sif/dot_general | solution.py:23
  98.2 2.5 %broadcast_in_dim.8 = f32[33,256,128]{2,1,0:T(8,128)} broadcast(f32[]{:T(128)} %constant.6.clone.1), dimensions={} | broadcast | bytes 4325380 | tf_op jit(solution)/shard_map/broadcast_in_dim | solution.py:27
  100.7 19.8 %scatter_fusion = f32[33,256,128]{2,1,0:T(8,128)} fusion(f32[33,256,128]{2,1,0:T(8,128)} %broadcast_in_dim.8, s32[64]{0:T(128)S(1)} %fusion.12, f32[64,256,128]{2,1,0:T(8,128)} %copy.13), kind=kCustom, calls=%fused_computation.1 | custom fusion | flops 2097152 | bytes 25166080 | tf_op jit(solution)/shard_map/scatter-add | solution.py:27
  120.5 4.6 %slice.10 = f32[32,256,128]{2,1,0:T(8,128)} slice(f32[33,256,128]{2,1,0:T(8,128)} %scatter_fusion), slice={[0:32], [0:256], [0:128]} | slice | bytes 8388608 | tf_op jit(solution)/shard_map/slice | solution.py:27
  125.1 0.0 reduce-scatter.2.cloned.1.call-update
  125.1 5.7 %convert_reduce_fusion = f32[64,256]{1,0:T(8,128)S(1)} fusion(bf16[1,1,64,256,256]{4,3,2,1,0:T(8,128)(2,1)} %param.9), kind=kLoop, calls=%fused_computation.3 | loop fusion | flops 8372224 | bytes 8454144 | tf_op jit(solution)/shard_map/reduce_sum | solution.py:30
  130.8 0.9 scatter_custom_fusion.1
  131.8 0.0 copy-done.4
  131.8 0.6 dynamic-slice
  133.1 27.0 %all-reduce = f32[8192]{0:T(1024)S(1)} all-reduce(f32[8192]{0:T(1024)S(1)} %bitcast.32), channel_id=3, replica_groups=mesh['row'=32,'col'=8] {'col'}, use_global_device_ids=true, to_apply=%region_4.5.clone | all-reduce | flops 8192 | bytes 65536
  160.0 0.0 copy-done
  160.0 0.3 fusion.13
  160.3 20.0 %reduce-scatter.2.cloned.1.call-done = f32[1024,128]{1,0:T(8,128)} async-done(((f32[8192,128]{1,0:T(8,128)}), f32[1024,128]{1,0:T(8,128)}) %reduce-scatter.2.cloned.1.call-update) | async-done | bytes 524304 | tf_op jit(solution)/shard_map/reduce_scatter | solution.py:35
  180.3 0.0 copy-done.2
  180.4 2.2 %fusion.7 = bf16[1024,256]{1,0:T(8,128)(2,1)} fusion(f32[1024,256]{1,0:T(8,128)S(1)} %fusion.13, bf16[128,256]{1,0:T(8,128)(2,1)S(1)} %copy-done.2, f32[256]{0:T(256)S(1)} %copy-done.3, f32[1024,128]{1,0:T(8,128)} %reduce-scatter.2.cloned.1.call-done, f32[1024]{0:T(1024)S(1)} %dynamic-slice_add_fusion), kind=kOutput, calls=%fused_computation.10 | convolution fusion | flops 68419584 | bytes 2167808 | tf_op jit(solution)/shard_map/dot_general | solution.py:39
  (10 shorter events, 0.0 us)
Async XLA Ops:
  6.5 153.5 %copy-start = (bf16[128,256]{1,0:T(8,128)(2,1)S(1)}, bf16[128,256]{1,0:T(8,128)(2,1)}, u32[]{:S(2)}) copy-start(bf16[128,256]{1,0:T(8,128)(2,1)} %param.13) | copy-start | bytes 196612
  6.5 65.5 %all-gather.2.cloned.1.call-start = ((), (), s32[]{:S(2)}) async-start(), calls=%async_computation.1 | async-start | bytes 8650752 | tf_op jit(solution)/shard_map/all_gather | solution.py:21
  7.3 173.1 %reduce-scatter.2.cloned.1.call-start = ((), (), s32[]{:S(2)}) async-start(), calls=%async_computation.2 | async-start | bytes 4718592 | tf_op jit(solution)/shard_map/reduce_scatter | solution.py:35
  125.1 6.7 %copy-start.4 = (u32[256]{0:T(256)S(1)}, u32[256]{0:T(256)}, u32[]{:S(2)}) copy-start(u32[256]{0:T(256)} %constant.22) | copy-start | bytes 3076
  125.1 34.9 %copy-start.1 = (bf16[1024,128]{1,0:T(8,128)(2,1)S(1)}, bf16[1024,128]{1,0:T(8,128)(2,1)}, u32[]{:S(2)}) copy-start(bf16[1024,128]{1,0:T(8,128)(2,1)} %param.8) | copy-start | bytes 786436
  125.1 55.2 %copy-start.2 = (bf16[128,256]{1,0:T(8,128)(2,1)S(1)}, bf16[128,256]{1,0:T(8,128)(2,1)}, u32[]{:S(2)}) copy-start(bf16[128,256]{1,0:T(8,128)(2,1)} %param.14) | copy-start | bytes 196612
  125.1 55.2 %copy-start.3 = (f32[256]{0:T(256)S(1)}, f32[256]{0:T(256)}, u32[]{:S(2)}) copy-start(f32[256]{0:T(256)} %param.15) | copy-start | bytes 3076
Sparse Core Ops, SparseCore 0:
  9.9 62.1 all-gather.1
  125.3 55.0 reduce-scatter.1

commit v2 on v1

v2 whole, which is shorter than its diff:
```python
import functools

import jax
import jax.numpy as jnp
from jax import lax
from jax.experimental import pallas as pl
from jax.experimental.pallas import tpu as pltpu
from jax.sharding import PartitionSpec as P

MESH = pl.DeviceIdType.MESH
F32, BF16 = jnp.float32, jnp.bfloat16

SIDE = 4
NZ = 8
BLK = 256
FEAT = 128
HID = 256
SLOTS = 64
DEST = 4
CHUNKS = 4
FC = FEAT // CHUNKS
GROUP = 16
UNROLL = 8
ONES = 16

COL, PREV, LAST = 0, SLOTS, 2 * SLOTS

N_GATHER = 13


def nt(a, b):
    return lax.dot_general(a, b, (((1,), (1,)), ((), ())), preferred_element_type=F32)


def tn(a, b):
    return lax.dot_general(a, b, (((0,), (0,)), ((), ())), preferred_element_type=F32)


def layer_kernel(
    plan,
    x_ref,
    adj_hbm,
    ws_ref,
    wn_ref,
    bias_ref,
    out_ref,
    *scratch,
):
    held = scratch[:CHUNKS]
    (
        tiles,
        sums,
        degs,
        rs_send,
        rs_recv,
        deg_send,
        deg_recv,
        mean_t,
        tile_sem,
        g_send,
        g_recv,
        r_send,
        r_recv,
        d_send,
        d_recv,
    ) = scratch[CHUNKS:]

    row, z = lax.axis_index("row"), lax.axis_index("col")
    k = row % 2
    cx, cy = row // (2 * SIDE), (row // 2) % SIDE
    i = (1 - k) * cx + k * cy
    j = (1 - k) * cy + k * cx

    def device(ii, jj):
        return (ii * (8 - 6 * k) + jj * (2 + 6 * k) + k, z)

    def place(kk, jj, ii):
        return kk * 16 + jj * 4 + ii

    ip, im, i2 = (i + 1) % SIDE, (i + 3) % SIDE, (i + 2) % SIDE
    jp, jm, j2 = (j + 1) % SIDE, (j + 3) % SIDE, (j + 2) % SIDE
    a_plus, a_minus = device(ip, j), device(im, j)
    b_plus, b_minus = device(i, jp), device(i, jm)
    sibling = (row + 1 - 2 * k, z)
    z_plus, z_minus = (row, (z + 1) % NZ), (row, (z + NZ - 1) % NZ)

    barrier = pltpu.get_barrier_semaphore()
    for peer in (a_plus, a_minus, b_plus, b_minus, sibling):
        pl.semaphore_signal(barrier, inc=1, device_id=peer, device_id_type=MESH)
    for off in range(1, NZ):
        pl.semaphore_signal(
            barrier, inc=1, device_id=(row, (z + off) % NZ), device_id_type=MESH
        )

    load = pltpu.make_async_copy(adj_hbm.at[0, 0], tiles, tile_sem)
    load.start()

    mine = place(k, j, i)
    for c in range(CHUNKS):
        eye = (
            lax.broadcasted_iota(jnp.int32, (FC, FEAT), 0) + c * FC
            == lax.broadcasted_iota(jnp.int32, (FC, FEAT), 1)
        ).astype(F32).astype(BF16)
        for b in range(DEST):
            held[c][mine, b] = nt(eye, x_ref[b * BLK : (b + 1) * BLK, :]).astype(BF16)

    sums[0, SLOTS] = jnp.zeros((FC, BLK), F32)
    sums[1, SLOTS] = jnp.zeros((FC, BLK), F32)
    degs[SLOTS] = jnp.zeros((8, BLK), F32)

    pl.semaphore_wait(barrier, 5 + NZ - 1)

    sent = []

    def send(c, n, ref, to):
        copy = pltpu.make_async_remote_copy(
            src_ref=ref,
            dst_ref=ref,
            send_sem=g_send.at[c, n],
            recv_sem=g_recv.at[c, n],
            device_id=to,
            device_id_type=MESH,
        )
        copy.start()
        sent.append(copy)

    def got(c, n, ref):
        pltpu.make_async_remote_copy(
            src_ref=ref,
            dst_ref=ref,
            send_sem=g_send.at[c, n],
            recv_sem=g_recv.at[c, n],
            device_id=sibling,
            device_id_type=MESH,
        ).wait_recv()

    def block(c, ii):
        return held[c].at[place(k, j, ii)]

    def block_half(c, ii, h):
        return held[c].at[place(k, j, ii), pl.ds(2 * h, 2)]

    def line(c, jj, kk=None):
        return held[c].at[pl.ds(place(k if kk is None else kk, jj, 0), 4)]

    def line_half(c, jj, h, kk=None):
        return held[c].at[pl.ds(place(k if kk is None else kk, jj, 2 * h), 2)]

    def first_axis_own(c):
        send(c, 0, block(c, i), a_plus)
        send(c, 1, block(c, i), a_minus)

    def first_axis_forward(c):
        got(c, 0, block(c, im))
        send(c, 2, block_half(c, im, 0), a_plus)
        got(c, 1, block(c, ip))
        send(c, 3, block_half(c, ip, 1), a_minus)

    def second_axis_own(c):
        got(c, 2, block_half(c, i2, 0))
        got(c, 3, block_half(c, i2, 1))
        send(c, 4, line(c, j), b_plus)
        send(c, 5, line(c, j), b_minus)
        send(c, 6, line(c, j), sibling)

    def second_axis_forward(c):
        got(c, 4, line(c, jm))
        send(c, 7, line_half(c, jm, 0), b_plus)
        send(c, 9, line(c, jm), sibling)
        got(c, 5, line(c, jp))
        send(c, 8, line_half(c, jp, 1), b_minus)
        send(c, 10, line(c, jp), sibling)

    def second_axis_end(c):
        got(c, 7, line_half(c, j2, 0))
        send(c, 11, line_half(c, j2, 0), sibling)
        got(c, 8, line_half(c, j2, 1))
        send(c, 12, line_half(c, j2, 1), sibling)
        other = 1 - k
        got(c, 6, line(c, i, other))
        got(c, 9, line(c, im, other))
        got(c, 10, line(c, ip, other))
        got(c, 11, line_half(c, i2, 0, other))
        got(c, 12, line_half(c, i2, 1, other))

    def compute(c, g):
        total = sums.at[c % 2]

        @pl.loop(0, GROUP // UNROLL)
        def _(step):
            for u in range(UNROLL):
                t = g * GROUP + step * UNROLL + u
                col = plan[COL + t]
                x = held[c][col // 4, col % 4]
                if c == 0:
                    x = jnp.concatenate([x, jnp.ones((ONES, BLK), BF16)], axis=0)
                res = nt(x, tiles[t])
                total[t] = res[:FC]
                if c == 0:
                    degs[t] = res[FC : FC + 8]

        @pl.loop(0, GROUP // UNROLL)
        def _(step):
            for u in range(UNROLL):
                t = g * GROUP + step * UNROLL + u
                prev = plan[PREV + t]
                total[t] = total[t] + total[prev]
                if c == 0:
                    degs[t] = degs[t] + degs[prev]

    def partial(c, dest, b):
        return sums[c % 2, plan[LAST + dest * DEST + b]]

    def ring(c, s):
        for way, to in ((0, z_plus), (1, z_minus)):
            dest = (z + (NZ // 2 - s if way == 0 else NZ // 2 + s)) % NZ
            first = range(0, 2) if way == 0 else range(2, 4)
            blocks = first if s == 0 else range(DEST)
            if s > 0:
                ring_got(c, way, s - 1)
            for b in blocks:
                val = partial(c, dest, b)
                if s > 1 or (s == 1 and b in first):
                    val = val + rs_recv[c, way, s - 1, b].astype(F32)
                rs_send[c, way, s, b] = val.astype(BF16)
            here = pl.ds(blocks[0], len(blocks))
            copy = pltpu.make_async_remote_copy(
                src_ref=rs_send.at[c, way, s, here],
                dst_ref=rs_recv.at[c, way, s, here],
                send_sem=r_send.at[c, way, s],
                recv_sem=r_recv.at[c, way, s],
                device_id=to,
                device_id_type=MESH,
            )
            copy.start()
            sent.append(copy)

    def ring_got(c, way, s):
        here = pl.ds(0 if s > 0 or way == 0 else 2, 2 if s == 0 else DEST)
        pltpu.make_async_remote_copy(
            src_ref=rs_send.at[c, way, s, here],
            dst_ref=rs_recv.at[c, way, s, here],
            send_sem=r_send.at[c, way, s],
            recv_sem=r_recv.at[c, way, s],
            device_id=z_plus,
            device_id_type=MESH,
        ).wait_recv()

    def send_degrees():
        for off in range(NZ):
            dest = (z + off) % NZ
            for b in range(DEST):
                deg_send[off, b : b + 1] = degs[plan[LAST + dest * DEST + b], 0:1]
            if off:
                copy = pltpu.make_async_remote_copy(
                    src_ref=deg_send.at[off],
                    dst_ref=deg_recv.at[off],
                    send_sem=d_send.at[off],
                    recv_sem=d_recv.at[off],
                    device_id=(row, dest),
                    device_id_type=MESH,
                )
                copy.start()
                sent.append(copy)

    def sum_degrees():
        total = 1.0 + deg_send[0]
        for off in range(1, NZ):
            pltpu.make_async_remote_copy(
                src_ref=deg_send.at[off],
                dst_ref=deg_recv.at[off],
                send_sem=d_send.at[off],
                recv_sem=d_recv.at[off],
                device_id=sibling,
                device_id_type=MESH,
            ).wait_recv()
            total = total + deg_recv[off]
        deg_send[0] = total

    def finish(c):
        ring_got(c, 0, 3)
        ring_got(c, 1, 3)
        for b in range(DEST):
            val = partial(c, z, b) + rs_recv[c, 0, 3, b].astype(F32) + rs_recv[c, 1, 3, b].astype(F32)
            val = val / deg_send[0, b : b + 1]
            mean_t[c * FC : (c + 1) * FC, b * BLK : (b + 1) * BLK] = val.astype(BF16)

    for c in range(CHUNKS):
        first_axis_own(c)
    for c in range(CHUNKS):
        first_axis_forward(c)
        if c < 2:
            second_axis_own(c)
    second_axis_forward(0)
    second_axis_own(2)
    load.wait()
    for c in range(CHUNKS):
        if c + 1 < CHUNKS:
            second_axis_forward(c + 1)
        if c + 3 < CHUNKS:
            second_axis_own(c + 3)
        second_axis_end(c)
        for g in range(SLOTS // GROUP):
            if c > 0:
                ring(c - 1, g)
            compute(c, g)
        if c == 0:
            send_degrees()
        if c == 1:
            sum_degrees()
        if c > 0:
            finish(c - 1)
    for s in range(4):
        ring(CHUNKS - 1, s)
    finish(CHUNKS - 1)

    for b in range(DEST):
        here = pl.ds(b * BLK, BLK)
        total = tn(mean_t[:, here], wn_ref[...])
        total = total + jnp.dot(x_ref[here, :], ws_ref[...], preferred_element_type=F32)
        total = total + bias_ref[...]
        out_ref[here, :] = jnp.maximum(total, 0.0).astype(BF16)

    for copy in sent:
        copy.wait_send()


def per_device(
    features, adjacency, block_rows, block_cols, live_counts, self_weight, neigh_weight, out_bias
):
    rows = block_rows[0, 0]
    t = jnp.arange(SLOTS)
    live = t < live_counts[0, 0]
    same = (rows[:, None] == rows[None, :]) & live[None, :] & (t[None, :] < t[:, None])
    prev = jnp.max(jnp.where(same, t[None, :], -1), axis=1)
    here = (jnp.arange(NZ * DEST)[:, None] == rows[None, :]) & live[None, :]
    last = jnp.max(jnp.where(here, t[None, :], -1), axis=1)
    cols = jnp.clip(block_cols[0, 0], 0, 32 * DEST - 1)
    dev, part = cols // DEST, cols % DEST
    core, cx, cy = dev % 2, dev // 8, (dev // 2) % 4
    spot = jnp.where(core == 0, cy * 4 + cx, 16 + cx * 4 + cy)
    plan = jnp.concatenate(
        [spot * DEST + part, jnp.where(prev < 0, SLOTS, prev), jnp.where(last < 0, SLOTS, last)]
    ).astype(jnp.int32)

    vmem = pl.BlockSpec(memory_space=pltpu.VMEM)
    dma = pltpu.SemaphoreType.DMA
    return pl.pallas_call(
        layer_kernel,
        out_shape=jax.ShapeDtypeStruct((DEST * BLK, HID), BF16),
        in_specs=[
            pl.BlockSpec(memory_space=pltpu.SMEM),
            vmem,
            pl.BlockSpec(memory_space=pl.ANY),
            vmem,
            vmem,
            vmem,
        ],
        out_specs=vmem,
        scratch_shapes=[pltpu.VMEM((32, DEST, FC, BLK), BF16) for _ in range(CHUNKS)]
        + [
            pltpu.VMEM((SLOTS, BLK, BLK), BF16),
            pltpu.VMEM((2, SLOTS + 1, FC, BLK), F32),
            pltpu.VMEM((SLOTS + 1, 8, BLK), F32),
            pltpu.VMEM((CHUNKS, 2, 4, DEST, FC, BLK), BF16),
            pltpu.VMEM((CHUNKS, 2, 4, DEST, FC, BLK), BF16),
            pltpu.VMEM((NZ, DEST, BLK), F32),
            pltpu.VMEM((NZ, DEST, BLK), F32),
            pltpu.VMEM((FEAT, DEST * BLK), BF16),
            dma,
            dma((CHUNKS, N_GATHER)),
            dma((CHUNKS, N_GATHER)),
            dma((CHUNKS, 2, 4)),
            dma((CHUNKS, 2, 4)),
            dma((NZ,)),
            dma((NZ,)),
        ],
        compiler_params=pltpu.CompilerParams(
            collective_id=0, has_side_effects=True, vmem_limit_bytes=48 * 2**20
        ),
    )(plan, features, adjacency, self_weight, neigh_weight, out_bias.reshape(1, HID))


def solution(mesh):
    in_specs = (
        P(("row", "col"), None),
        P("row", "col", None, None, None),
        P("row", "col", None),
        P("row", "col", None),
        P("row", "col"),
        P(),
        P(),
        P(),
    )
    out_specs = P(("row", "col"), None)
    return jax.shard_map(
        per_device, mesh=mesh, in_specs=in_specs, out_specs=out_specs, check_vma=False
    )
```

time: 190 us -> 104 us (0.55)
  the two profiles are of different devices: /device:TPU:1 before, /device:TPU:32 now
where the time goes in v2:
time: 104 us
  Pallas kernels  96.3 us (93%)
  local copies, waits for them, and re-layouts  4.1 us (4%)
  other arithmetic  2.48 us (2%)
    pallas_call x1, Pallas kernels, per_device(): pl.pallas_call(layer_kernel, out_shape=jax.ShapeDtypeStruct((DEST * BLK,...  96.3 us
    unnamed x9, local copies, waits for them, and re-layouts  4.1 us

profile of v2, /device:TPU:32, one launch (start us, length us, event | category | flops | bytes accessed | tf_op | source)
XLA Modules:
  0.0 103.6 jit_solution(13275548889360287755)
XLA Ops:
  0.7 0.9 select_reduce_fusion
  1.6 0.8 select_reduce_fusion.1
  2.4 0.7 compare_select_fusion.1
  3.1 0.1 pad_add_fusion.plan
  3.1 0.0 copy-start
  3.1 0.9 copy-done
  4.1 0.0 copy-start.1
  4.1 0.8 copy-done.1
  4.9 0.0 copy-start.2
  4.9 0.8 copy-done.2
  5.8 0.0 copy-start.3
  5.8 0.7 copy-done.3
  6.5 96.3 %shard_map.82 = bf16[1024,256]{1,0:T(8,128)(2,1)S(1)} custom-call(s32[160]{0:T(256)S(1)} %pad_add_fusion.plan, bf16[1024,128]{1,0:T(8,128)(2,1)S(1)} %copy-done, bf16[1,1,64,256,256]{4,3,2,1,0:T(8,128)(2,1)} %adj_hbm.1, bf16[128,256]{1,0:T(8,128)(2,1)S(1)} %copy-done.1, bf16[128,256]{1,0:T(8,128)(2,1)S(1)} %copy-done.2, f32[1,256]{1,0:T(1,128)S(1)} %bitcast.17), custom_call_target="tpu_custom_call" | custom-call | tf_op jit(solution)/shard_map/pallas_call | solution.py:348
  102.8 0.8 copy.11
  (2 shorter events, 0.0 us)
Async XLA Ops:
  3.1 0.9 copy-start
  4.1 0.8 copy-start.1
  4.9 0.8 copy-start.2
  5.8 0.7 copy-start.3

commit v3 on v1

v3 whole, which is shorter than its diff:
```python
import functools

import jax
import jax.numpy as jnp
from jax import lax
from jax.experimental import pallas as pl
from jax.experimental.pallas import tpu as pltpu
from jax.sharding import PartitionSpec as P

MESH = pl.DeviceIdType.MESH
F32, BF16, I32 = jnp.float32, jnp.bfloat16, jnp.int32

SIDE = 4
NZ = 8
HOPS = NZ // 2
BLK = 256
FEAT = 128
HID = 256
SLOTS = 64
DEST = 4
SUB = SIDE * DEST
SIZES = (48, 32, 32, 16)
CHUNKS = len(SIZES)
STARTS = tuple(sum(SIZES[:c]) for c in range(CHUNKS))
DIRECT = (False, False, False, False)
TREE = (False, False, False, True)
PARTS = 4
ORDER = (
    ("own", 1), ("own", 0), ("ff0", 1), ("ff1", 1), ("own", 2), ("of0", 1),
    ("of1", 1), ("ff0", 0), ("ff1", 0), ("own", 3), ("of0", 0), ("ro", 1),
    ("of0", 2), ("ro", 0), ("of1", 3), ("rf1", 1), ("rf0", 1), ("ff1", 2),
    ("ff0", 2), ("of1", 0), ("of1", 2), ("ff1", 3), ("of0", 3), ("ff0", 3),
    ("rf1", 0), ("rf0", 0), ("far", 1), ("ro", 2), ("ro", 3), ("sib", 1),
    ("comp0", 1), ("comp1", 1), ("comp2", 1), ("far", 0), ("comp3", 1), ("ring0", 1),
    ("rf0", 2), ("rf1", 2), ("sib", 0), ("comp0", 0), ("comp1", 0), ("comp2", 0),
    ("comp3", 0), ("far", 2), ("ring0", 0), ("rf1", 3), ("rf0", 3), ("ring1", 1),
    ("sib", 2), ("comp0", 2), ("comp1", 2), ("comp2", 2), ("comp3", 2), ("ring0", 2),
    ("far", 3), ("ring1", 0), ("ring2", 1), ("sib", 3), ("comp0", 3), ("comp1", 3),
    ("comp2", 3), ("ring1", 2), ("comp3", 3), ("t0", 3), ("t1", 3), ("ring2", 0),
    ("ring3", 1), ("ring2", 2), ("t2", 3), ("ring3", 0), ("fin", 1), ("ring3", 2),
    ("fin", 3), ("fin", 0), ("fin", 2),
)
LEAD = 1
UNROLL = 16
ONES = 16
LANES = 128
SPOT, PREV, LAST = 0, 1, 2
N_GATHER = 16


def nt(a, b):
    return lax.dot_general(a, b, (((1,), (1,)), ((), ())), preferred_element_type=F32)


def tn(a, b):
    return lax.dot_general(a, b, (((0,), (0,)), ((), ())), preferred_element_type=F32)


def layer_kernel(
    counts,
    rows_ref,
    cols_ref,
    x_hbm,
    adj_hbm,
    ws_hbm,
    wn_hbm,
    bias_hbm,
    out_ref,
    *scratch,
):
    held, scratch = scratch[:CHUNKS], scratch[CHUNKS:]
    sums, scratch = scratch[:CHUNKS], scratch[CHUNKS:]
    rs_send, scratch = scratch[:CHUNKS], scratch[CHUNKS:]
    rs_recv, scratch = scratch[:CHUNKS], scratch[CHUNKS:]
    (
        tiles,
        degs,
        deg_send,
        deg_recv,
        degree,
        x_ref,
        ws_ref,
        wn_ref,
        bias_ref,
        acc,
        plan_v,
        plan,
        tile_sem,
        in_sem,
        g_send,
        g_recv,
        r_send,
        r_recv,
        d_send,
        d_recv,
    ) = scratch

    row, z = lax.axis_index("row"), lax.axis_index("col")
    k = row % 2
    cx, cy = row // (2 * SIDE), (row // 2) % SIDE
    i = (1 - k) * cx + k * cy
    j = (1 - k) * cy + k * cx

    def device(ii, jj):
        return (ii * (8 - 6 * k) + jj * (2 + 6 * k) + k, z)

    ip, im, i2 = (i + 1) % SIDE, (i + 3) % SIDE, (i + 2) % SIDE
    jp, jm, j2 = (j + 1) % SIDE, (j + 3) % SIDE, (j + 2) % SIDE
    a_plus, a_minus, a_far = device(ip, j), device(im, j), device(i2, j)
    b_plus, b_minus, b_far = device(i, jp), device(i, jm), device(i, j2)
    sibling = (row + 1 - 2 * k, z)
    z_plus, z_minus = (row, (z + 1) % NZ), (row, (z + NZ - 1) % NZ)
    z_plus2, z_minus2 = (row, (z + 2) % NZ), (row, (z + NZ - 2) % NZ)

    barrier = pltpu.get_barrier_semaphore()
    peers = [a_plus, a_minus, b_plus, b_minus, sibling, z_plus, z_minus]
    if any(DIRECT):
        peers += [a_far, b_far]
    if any(TREE):
        peers += [z_plus2, z_minus2]
    for peer in peers:
        pl.semaphore_signal(barrier, inc=1, device_id=peer, device_id_type=MESH)

    loads = [
        pltpu.make_async_copy(src, dst, in_sem.at[n])
        for n, (src, dst) in enumerate(
            ((x_hbm, x_ref), (ws_hbm, ws_ref), (wn_hbm, wn_ref), (bias_hbm, bias_ref))
        )
    ]
    for load in loads:
        load.start()
    tile_load = pltpu.make_async_copy(adj_hbm.at[0, 0], tiles, tile_sem)
    tile_load.start()

    loads[0].wait()
    for c in range(CHUNKS):
        eye = (
            lax.broadcasted_iota(I32, (SIZES[c], FEAT), 0) + STARTS[c]
            == lax.broadcasted_iota(I32, (SIZES[c], FEAT), 1)
        ).astype(F32).astype(BF16)
        for b in range(DEST):
            held[c][k, j, b] = nt(eye, x_ref[b * BLK : (b + 1) * BLK, :]).astype(BF16)

    pl.semaphore_wait(barrier, len(peers))

    sent = []

    def send(c, n, src, dst, to):
        copy = pltpu.make_async_remote_copy(
            src_ref=src,
            dst_ref=dst,
            send_sem=g_send.at[c, n],
            recv_sem=g_recv.at[c, n],
            device_id=to,
            device_id_type=MESH,
        )
        copy.start()
        sent.append(copy)

    def got(c, n, ref):
        pltpu.make_async_remote_copy(
            src_ref=ref,
            dst_ref=ref,
            send_sem=g_send.at[c, n],
            recv_sem=g_recv.at[c, n],
            device_id=sibling,
            device_id_type=MESH,
        ).wait_recv()

    def part(c, jj, lo, n, kk=None):
        return held[c].at[k if kk is None else kk, jj, pl.ds(lo, n)]

    def own_out(c):
        mine = part(c, j, 0, 4)
        send(c, 0, mine, part(c, j, 12, 4), a_plus)
        send(c, 1, mine, part(c, j, 4, 4), a_minus)
        if DIRECT[c]:
            send(c, 2, mine, part(c, j, 8, 4), a_far)
        send(c, 4, mine, mine, b_plus)
        send(c, 5, mine, mine, b_minus)
        if DIRECT[c]:
            send(c, 6, mine, mine, b_far)

    def first_forward(c, way):
        if way == 0:
            got(c, 0, part(c, j, 12, 4))
            if not DIRECT[c]:
                send(c, 2, part(c, j, 12, 2), part(c, j, 8, 2), a_plus)
        else:
            got(c, 1, part(c, j, 4, 4))
            if not DIRECT[c]:
                send(c, 3, part(c, j, 6, 2), part(c, j, 10, 2), a_minus)

    def own_forward(c, way):
        if way == 0:
            got(c, 4, part(c, jm, 0, 4))
            if not DIRECT[c]:
                send(c, 6, part(c, jm, 0, 2), part(c, jm, 0, 2), b_plus)
        else:
            got(c, 5, part(c, jp, 0, 4))
            if not DIRECT[c]:
                send(c, 7, part(c, jp, 2, 2), part(c, jp, 2, 2), b_minus)

    def rest_out(c):
        if DIRECT[c]:
            got(c, 2, part(c, j, 8, 4))
        else:
            got(c, 2, part(c, j, 8, 2))
            got(c, 3, part(c, j, 10, 2))
        rest = part(c, j, 4, 12)
        send(c, 8, rest, rest, b_plus)
        send(c, 9, rest, rest, b_minus)
        if DIRECT[c]:
            send(c, 10, rest, rest, b_far)
        line = part(c, j, 0, SUB)
        send(c, 12, line, line, sibling)

    def rest_forward(c, way):
        if way == 0:
            got(c, 8, part(c, jm, 4, 12))
            if not DIRECT[c]:
                send(c, 10, part(c, jm, 4, 6), part(c, jm, 4, 6), b_plus)
            line = part(c, jm, 0, SUB)
            send(c, 13, line, line, sibling)
        else:
            got(c, 9, part(c, jp, 4, 12))
            if not DIRECT[c]:
                send(c, 11, part(c, jp, 10, 6), part(c, jp, 10, 6), b_minus)
            line = part(c, jp, 0, SUB)
            send(c, 14, line, line, sibling)

    def far_in(c):
        if DIRECT[c]:
            got(c, 6, part(c, j2, 0, 4))
            got(c, 10, part(c, j2, 4, 12))
        else:
            got(c, 6, part(c, j2, 0, 2))
            got(c, 7, part(c, j2, 2, 2))
            got(c, 10, part(c, j2, 4, 6))
            got(c, 11, part(c, j2, 10, 6))
        line = part(c, j2, 0, SUB)
        send(c, 15, line, line, sibling)

    def sibling_in(c):
        for n, jj in ((12, i), (13, im), (14, ip), (15, i2)):
            got(c, n, part(c, jj, 0, SUB, 1 - k))

    def make_plan():
        t = lax.broadcasted_iota(I32, (LANES, LANES), 1)
        s = lax.broadcasted_iota(I32, (LANES, LANES), 0)
        plan_v[...] = jnp.zeros((8, LANES), I32)
        plan_v[0:1, 0:SLOTS] = rows_ref[0]
        along = jnp.broadcast_to(plan_v[0:1, :], (LANES, LANES))
        down = jnp.transpose(along)
        live = s < counts[0, 0]
        prev = jnp.max(jnp.where((along == down) & live & (s < t), s, -1), axis=0, keepdims=True)
        last = jnp.max(jnp.where((down == t) & live, s, -1), axis=0, keepdims=True)
        plan_v[0:1, 0:SLOTS] = cols_ref[0]
        cols = jnp.clip(plan_v[0:1, :], 0, 32 * DEST - 1)
        dev = cols // DEST
        ox, oy, core = dev // 8, (dev // 2) % SIDE, dev % 2
        oi = jnp.where(core == 0, ox - cx, oy - cy)
        oj = jnp.where(core == 0, oy, ox)
        plan_v[SPOT : SPOT + 1, :] = core * 64 + oj * SUB + (oi + SIDE) % SIDE * DEST + cols % DEST
        plan_v[PREV : PREV + 1, :] = jnp.where(prev < 0, SLOTS, prev)
        plan_v[LAST : LAST + 1, :] = jnp.where(last < 0, SLOTS, last)
        move = pltpu.make_async_copy(plan_v, plan, in_sem.at[4])
        move.start()
        move.wait()

    def own_part():
        for load in loads[1:]:
            load.wait()
        for b in range(DEST):
            here = pl.ds(b * BLK, BLK)
            own = jnp.dot(x_ref[here, :], ws_ref[...], preferred_element_type=F32)
            acc[here, :] = own + bias_ref[...]

    def compute(c, q):
        total, size = sums[c], SIZES[c]
        steps = SLOTS // PARTS // UNROLL

        @pl.loop(q * steps, (q + 1) * steps)
        def _(step):
            for u in range(UNROLL):
                t = step * UNROLL + u
                spot = plan[SPOT, t]
                x = held[c][spot // 64, spot // SUB % SIDE, spot % SUB]
                if c == LEAD:
                    x = jnp.concatenate([x, jnp.ones((ONES, BLK), BF16)], axis=0)
                res = nt(x, tiles[t])
                total[t] = res[:size]
                if c == LEAD:
                    degs[t] = res[size : size + 8]
            for u in range(UNROLL):
                t = step * UNROLL + u
                prev = plan[PREV, t]
                total[t] = total[t] + total[prev]
                if c == LEAD:
                    degs[t] = degs[t] + degs[prev]

    def partial(c, dest, b):
        return sums[c][plan[LAST, dest * DEST + b]]

    def degree_row(dest, b):
        return degs[plan[LAST, dest * DEST + b], 0:1]

    def ring_send(c, way, s, lo, n, to):
        here = pl.ds(lo, n)
        copy = pltpu.make_async_remote_copy(
            src_ref=rs_send[c].at[way, s, here],
            dst_ref=rs_recv[c].at[way, s, here],
            send_sem=r_send.at[c, way, s],
            recv_sem=r_recv.at[c, way, s],
            device_id=to,
            device_id_type=MESH,
        )
        copy.start()
        sent.append(copy)

    def ring(c, s):
        for way, to in ((0, z_plus), (1, z_minus)):
            dest = (z + (HOPS - s if way == 0 else HOPS + s)) % NZ
            first = range(0, 2) if way == 0 else range(2, 4)
            blocks = first if s == 0 else range(DEST)
            if s > 0:
                ring_got(c, way, s - 1, 2 if s == 1 else DEST)
            for b in blocks:
                val = partial(c, dest, b)
                if s > 1 or (s == 1 and b in first):
                    val = val + rs_recv[c][way, s - 1, b].astype(F32)
                rs_send[c][way, s, b] = val.astype(BF16)
            ring_send(c, way, s, blocks[0], len(blocks), to)
            if c == LEAD:
                degree_send(way, s, dest, blocks, (s - 1,) if s > 0 else (), to)

    def degree_send(way, s, dest, blocks, arrived, to):
        for b in range(DEST):
            val = degree_row(dest, b) if b in blocks else jnp.zeros((1, BLK), F32)
            for n in arrived:
                val = val + deg_recv[way, n, b : b + 1]
            deg_send[way, s, b : b + 1] = val
        copy = degree_copy(way, s, to)
        copy.start()
        sent.append(copy)

    def tree(c, stage):
        for way, to, to2 in ((0, z_plus, z_plus2), (1, z_minus, z_minus2)):
            sign = 1 if way == 0 else NZ - 1
            half = 2 * way
            if stage == 0:
                for b in range(DEST):
                    rs_send[c][way, 0, b] = partial(c, (z + 3 * sign) % NZ, b).astype(BF16)
                ring_send(c, way, 0, 0, DEST, to)
                if c == LEAD:
                    degree_send(way, 0, (z + 3 * sign) % NZ, range(DEST), (), to)
                for b in range(half, half + 2):
                    rs_send[c][way, 1, b] = partial(c, (z + 4) % NZ, b).astype(BF16)
                ring_send(c, way, 1, half, 2, to2)
                if c == LEAD:
                    degree_send(way, 1, (z + 4) % NZ, range(half, half + 2), (), to2)
            elif stage == 1:
                for b in range(DEST):
                    rs_send[c][way, 2, b] = partial(c, (z + sign) % NZ, b).astype(BF16)
                ring_send(c, way, 2, 0, DEST, to)
                if c == LEAD:
                    degree_send(way, 2, (z + sign) % NZ, range(DEST), (), to)
            else:
                ring_got(c, way, 0, DEST)
                ring_got(c, way, 1, 2)
                for b in range(DEST):
                    val = partial(c, (z + 2 * sign) % NZ, b) + rs_recv[c][way, 0, b].astype(F32)
                    if b in (half, half + 1):
                        val = val + rs_recv[c][way, 1, b].astype(F32)
                    rs_send[c][way, 3, b] = val.astype(BF16)
                ring_send(c, way, 3, 0, DEST, to2)
                if c == LEAD:
                    degree_send(way, 3, (z + 2 * sign) % NZ, range(DEST), (0, 1), to2)

    def degree_copy(way, s, to):
        return pltpu.make_async_remote_copy(
            src_ref=deg_send.at[way, s],
            dst_ref=deg_recv.at[way, s],
            send_sem=d_send.at[way, s],
            recv_sem=d_recv.at[way, s],
            device_id=to,
            device_id_type=MESH,
        )

    def ring_got(c, way, s, n):
        here = pl.ds(2 * way if n == 2 else 0, n)
        pltpu.make_async_remote_copy(
            src_ref=rs_send[c].at[way, s, here],
            dst_ref=rs_recv[c].at[way, s, here],
            send_sem=r_send.at[c, way, s],
            recv_sem=r_recv.at[c, way, s],
            device_id=z_plus,
            device_id_type=MESH,
        ).wait_recv()
        if c == LEAD:
            degree_copy(way, s, z_plus).wait_recv()

    def finish(c, final):
        arrived = (2, 3) if TREE[c] else (3,)
        for way in range(2):
            for s in arrived:
                ring_got(c, way, s, DEST)
        for b in range(DEST):
            if c == LEAD:
                mine = 1.0 + degree_row(z, b)
                for way in range(2):
                    for s in arrived:
                        mine = mine + deg_recv[way, s, b : b + 1]
                degree[b : b + 1] = mine
            val = partial(c, z, b)
            for way in range(2):
                for s in arrived:
                    val = val + rs_recv[c][way, s, b].astype(F32)
            mean = (val / degree[b : b + 1]).astype(BF16)
            here = pl.ds(b * BLK, BLK)
            total = acc[here, :] + tn(mean, wn_ref[STARTS[c] : STARTS[c] + SIZES[c], :])
            if final:
                out_ref[here, :] = jnp.maximum(total, 0.0).astype(BF16)
            else:
                acc[here, :] = total

    def prepare():
        for c in range(CHUNKS):
            sums[c][SLOTS] = jnp.zeros((SIZES[c], BLK), F32)
        degs[SLOTS] = jnp.zeros((8, BLK), F32)
        make_plan()
        own_part()

    run = {
        "own": own_out,
        "ff0": lambda c: first_forward(c, 0),
        "ff1": lambda c: first_forward(c, 1),
        "of0": lambda c: own_forward(c, 0),
        "of1": lambda c: own_forward(c, 1),
        "ro": rest_out,
        "rf0": lambda c: rest_forward(c, 0),
        "rf1": lambda c: rest_forward(c, 1),
        "far": far_in,
        "sib": sibling_in,
    }
    for q in range(PARTS):
        run[f"comp{q}"] = functools.partial(compute, q=q)
    for s in range(HOPS):
        run[f"ring{s}"] = functools.partial(ring, s=s)
    for stage in range(3):
        run[f"t{stage}"] = functools.partial(tree, stage=stage)
    final = [n for n, (name, _) in enumerate(ORDER) if name == "fin"][-1]
    ready = loaded = False
    for n, (name, c) in enumerate(ORDER):
        if name == "comp0" and not loaded:
            tile_load.wait()
            loaded = True
        if name != "own" and not ready:
            prepare()
            ready = True
        if name == "fin":
            finish(c, n == final)
        else:
            run[name](c)

    for copy in sent:
        copy.wait_send()


def per_device(
    features, adjacency, block_rows, block_cols, live_counts, self_weight, neigh_weight, out_bias
):
    vmem = pl.BlockSpec(memory_space=pltpu.VMEM)
    smem = pl.BlockSpec(memory_space=pltpu.SMEM)
    hbm = pl.BlockSpec(memory_space=pltpu.HBM)
    dma = pltpu.SemaphoreType.DMA
    return pl.pallas_call(
        layer_kernel,
        out_shape=jax.ShapeDtypeStruct((DEST * BLK, HID), BF16),
        in_specs=[smem, vmem, vmem, hbm, hbm, hbm, hbm, hbm],
        out_specs=vmem,
        scratch_shapes=[pltpu.VMEM((2, SIDE, SUB, size, BLK), BF16) for size in SIZES]
        + [pltpu.VMEM((SLOTS + 1, size, BLK), F32) for size in SIZES]
        + [pltpu.VMEM((2, HOPS, DEST, size, BLK), BF16) for size in SIZES]
        + [pltpu.VMEM((2, HOPS, DEST, size, BLK), BF16) for size in SIZES]
        + [
            pltpu.VMEM((SLOTS, BLK, BLK), BF16),
            pltpu.VMEM((SLOTS + 1, 8, BLK), F32),
            pltpu.VMEM((2, HOPS, DEST, BLK), F32),
            pltpu.VMEM((2, HOPS, DEST, BLK), F32),
            pltpu.VMEM((DEST, BLK), F32),
            pltpu.VMEM((DEST * BLK, FEAT), BF16),
            pltpu.VMEM((FEAT, HID), BF16),
            pltpu.VMEM((FEAT, HID), BF16),
            pltpu.VMEM((1, HID), F32),
            pltpu.VMEM((DEST * BLK, HID), F32),
            pltpu.VMEM((8, LANES), I32),
            pltpu.SMEM((8, LANES), I32),
            dma,
            dma((5,)),
            dma((CHUNKS, N_GATHER)),
            dma((CHUNKS, N_GATHER)),
            dma((CHUNKS, 2, HOPS)),
            dma((CHUNKS, 2, HOPS)),
            dma((2, HOPS)),
            dma((2, HOPS)),
        ],
        compiler_params=pltpu.CompilerParams(
            collective_id=0, has_side_effects=True, vmem_limit_bytes=56 * 2**20
        ),
    )(
        live_counts,
        block_rows,
        block_cols,
        features,
        adjacency,
        self_weight,
        neigh_weight,
        out_bias.reshape(1, HID),
    )


def solution(mesh):
    in_specs = (
        P(("row", "col"), None),
        P("row", "col", None, None, None),
        P("row", "col", None),
        P("row", "col", None),
        P("row", "col"),
        P(),
        P(),
        P(),
    )
    out_specs = P(("row", "col"), None)
    return jax.shard_map(
        per_device, mesh=mesh, in_specs=in_specs, out_specs=out_specs, check_vma=False
    )
```

time: 190 us -> 67.1 us (0.35)
  waiting for transfers between devices: 83.6 us -> 0 us
  Pallas kernels: 0 us -> 64.5 us
  other arithmetic: 27.8 us -> 0 us
  blocking collectives: 27 us -> 0 us
  local copies, waits for them, and re-layouts: 23.1 us -> 1.87 us
  between operations: 14.8 us -> 0.66 us
  matrix products: 13.2 us -> 0 us
    pallas_call x0 -> x1, Pallas kernels: none -> 64.5 us  [per_device(): pl.pallas_call(layer_kernel, out_shape=jax.ShapeDtypeStruct((DEST * BLK,...]
    all_gather x1 -> x0, waiting for transfers between devices: 62.8 us -> none  [per_device(): column_x = lax.all_gather(features, 'row', axis=0, tiled=True)]
    unnamed x1 -> x0, blocking collectives: 27 us -> none
    scatter-add x2 -> x0, other arithmetic: 20.8 us -> none  [the longest x1 19.8 us: per_device(): jnp.zeros((row_blocks + 1, block, feat), jnp.float32).at[target]]
    reduce_scatter x1 -> x0, waiting for transfers between devices: 20 us -> none  [per_device(): lax.psum_scatter(partial_value, 'col', scatter_dimension=0, tiled=True)]
    dot_general x3 -> x0, matrix products: 13.2 us -> none  [the longest x1 10.8 us: per_device(): jnp.einsum('sij,sjf->sif', tile, picked, preferred_element_type=jnp.float32)]
    dot_general x1 -> x0, local copies, waits for them, and re-layouts: 8.99 us -> none  [per_device(): jnp.einsum('sij,sjf->sif', tile, picked, preferred_element_type=jnp.float32)]
    gather x1 -> x0, local copies, waits for them, and re-layouts: 6.39 us -> none  [per_device(): picked = column_x.reshape(col_blocks, block, feat)[cols_here]]
  transfers between devices with their start and end apart: 2 -> 0, of which waited for: 2 -> 0; matrix products, arithmetic and copies ran while one was open for 5% -> 0% of each run, Pallas kernels for 0% -> 0%
where the time goes in v3:
time: 67.1 us; the launch traced here: 67 us
  Pallas kernels  64.5 us (96%)
  local copies, waits for them, and re-layouts  1.87 us (3%)
    pallas_call x1, Pallas kernels, per_device(): pl.pallas_call(layer_kernel, out_shape=jax.ShapeDtypeStruct((DEST * BLK,...  64.5 us
    unnamed x1, local copies, waits for them, and re-layouts  1.87 us

profile of v3, /device:TPU:1, one launch (start us, length us, event | category | flops | bytes accessed | tf_op | source)
XLA Modules:
  0.0 67.0 jit_solution(6331245942755189467)
XLA Ops:
  0.7 64.5 %shard_map.82 = bf16[1024,256]{1,0:T(8,128)(2,1)} custom-call(s32[1,1]{1,0:T(1,128)S(6)} %copy.10.counts, s32[1,1,64]{2,1,0:T(1,128)} %rows_ref.1, s32[1,1,64]{2,1,0:T(1,128)} %cols_ref.1, bf16[1024,128]{1,0:T(8,128)(2,1)} %x_hbm.1, bf16[1,1,64,256,256]{4,3,2,1,0:T(8,128)(2,1)} %adj_hbm.1, bf16[128,256]{1,0:T(8,128)(2,1)} %ws_hbm.1, ...), custom_call_target="tpu_custom_call" | custom-call | tf_op jit(solution)/shard_map/pallas_call | solution.py:477
  65.1 1.9 %copy.11 = bf16[1024,256]{1,0:T(8,128)(2,1)} copy(bf16[1024,256]{1,0:T(8,128)(2,1)} %shard_map.82) | data formatting | bytes 1048576

commit v4 on v3

--- a/solution.py
+++ b/solution.py
@@ -19,28 +19,25 @@
 SLOTS = 64
 DEST = 4
 SUB = SIDE * DEST
-SIZES = (48, 32, 32, 16)
+SIZES = (48, 48, 32)
 CHUNKS = len(SIZES)
 STARTS = tuple(sum(SIZES[:c]) for c in range(CHUNKS))
-DIRECT = (False, False, False, False)
-TREE = (False, False, False, True)
+DIRECT = (False, False, False)
+TREE = (False, False, True)
 PARTS = 4
 ORDER = (
-    ("own", 1), ("own", 0), ("ff0", 1), ("ff1", 1), ("own", 2), ("of0", 1),
-    ("of1", 1), ("ff0", 0), ("ff1", 0), ("own", 3), ("of0", 0), ("ro", 1),
-    ("of0", 2), ("ro", 0), ("of1", 3), ("rf1", 1), ("rf0", 1), ("ff1", 2),
-    ("ff0", 2), ("of1", 0), ("of1", 2), ("ff1", 3), ("of0", 3), ("ff0", 3),
-    ("rf1", 0), ("rf0", 0), ("far", 1), ("ro", 2), ("ro", 3), ("sib", 1),
-    ("comp0", 1), ("comp1", 1), ("comp2", 1), ("far", 0), ("comp3", 1), ("ring0", 1),
-    ("rf0", 2), ("rf1", 2), ("sib", 0), ("comp0", 0), ("comp1", 0), ("comp2", 0),
-    ("comp3", 0), ("far", 2), ("ring0", 0), ("rf1", 3), ("rf0", 3), ("ring1", 1),
-    ("sib", 2), ("comp0", 2), ("comp1", 2), ("comp2", 2), ("comp3", 2), ("ring0", 2),
-    ("far", 3), ("ring1", 0), ("ring2", 1), ("sib", 3), ("comp0", 3), ("comp1", 3),
-    ("comp2", 3), ("ring1", 2), ("comp3", 3), ("t0", 3), ("t1", 3), ("ring2", 0),
-    ("ring3", 1), ("ring2", 2), ("t2", 3), ("ring3", 0), ("fin", 1), ("ring3", 2),
-    ("fin", 3), ("fin", 0), ("fin", 2),
+    ("own", 2), ("own", 1), ("ff0", 2), ("ff1", 2), ("own", 0), ("of1", 2),
+    ("of0", 2), ("ff0", 1), ("ff1", 1), ("of0", 1), ("of1", 1), ("ro", 2),
+    ("ff1", 0), ("ff0", 0), ("ro", 1), ("rf0", 2), ("rf1", 2), ("ro", 0),
+    ("rf0", 1), ("far", 2), ("rf1", 1), ("sib", 2), ("comp0", 2), ("of0", 0),
+    ("comp1", 2), ("comp2", 2), ("of1", 0), ("rf0", 0), ("comp3", 2), ("far", 1),
+    ("rf1", 0), ("t0", 2), ("t1", 2), ("sib", 1), ("comp0", 1), ("comp1", 1),
+    ("comp2", 1), ("far", 0), ("comp3", 1), ("ring0", 1), ("sib", 0), ("comp0", 0),
+    ("comp1", 0), ("t2", 2), ("comp2", 0), ("comp3", 0), ("ring0", 0), ("ring1", 1),
+    ("fin", 2), ("ring1", 0), ("ring2", 1), ("ring2", 0), ("ring3", 1), ("ring3", 0),
+    ("fin", 1), ("fin", 0),
 )
-LEAD = 1
+LEAD = 2
 UNROLL = 16
 ONES = 16
 LANES = 128
@@ -476,7 +473,7 @@
     dma = pltpu.SemaphoreType.DMA
     return pl.pallas_call(
         layer_kernel,
-        out_shape=jax.ShapeDtypeStruct((DEST * BLK, HID), BF16),
+        out_shape=pltpu.VMEM((DEST * BLK, HID), BF16),
         in_specs=[smem, vmem, vmem, hbm, hbm, hbm, hbm, hbm],
         out_specs=vmem,
         scratch_shapes=[pltpu.VMEM((2, SIDE, SUB, size, BLK), BF16) for size in SIZES]

time: 67.1 us -> 61.7 us (0.920)
  Pallas kernels: 64.5 us -> 60 us
  local copies, waits for them, and re-layouts: 1.87 us -> 0.8 us
    pallas_call x1, Pallas kernels: 64.5 us -> 60 us  [per_device(): pl.pallas_call(layer_kernel, out_shape=pltpu.VMEM((DEST * BLK, HID), BF16...]
    unnamed x1, local copies, waits for them, and re-layouts: 1.87 us -> 0.8 us
where the time goes in v4:
time: 61.7 us; the launch traced here: 61.4 us
  Pallas kernels  60 us (97%)
  local copies, waits for them, and re-layouts  0.8 us (1%)
  between operations  0.66 us (1%)
    pallas_call x1, Pallas kernels, per_device(): pl.pallas_call(layer_kernel, out_shape=pltpu.VMEM((DEST * BLK, HID), BF16...  60 us

profile of v4, /device:TPU:1, one launch (start us, length us, event | category | flops | bytes accessed | tf_op | source)
XLA Modules:
  0.0 61.4 jit_solution(4974357330483949678)
XLA Ops:
  0.7 60.0 %shard_map.82 = bf16[1024,256]{1,0:T(8,128)(2,1)S(1)} custom-call(s32[1,1]{1,0:T(1,128)S(6)} %copy.11.counts, s32[1,1,64]{2,1,0:T(1,128)} %rows_ref.1, s32[1,1,64]{2,1,0:T(1,128)} %cols_ref.1, bf16[1024,128]{1,0:T(8,128)(2,1)} %x_hbm.1, bf16[1,1,64,256,256]{4,3,2,1,0:T(8,128)(2,1)} %adj_hbm.1, bf16[128,256]{1,0:T(8,128)(2,1)} %ws_hbm.1, ...), custom_call_target="tpu_custom_call" | custom-call | tf_op jit(solution)/shard_map/pallas_call | solution.py:474
  60.6 0.8 %copy.10 = bf16[1024,256]{1,0:T(8,128)(2,1)} copy(bf16[1024,256]{1,0:T(8,128)(2,1)S(1)} %shard_map.82) | data formatting | bytes 1048576

commit v5 on v4

--- a/solution.py
+++ b/solution.py
@@ -129,8 +129,7 @@
     tile_load = pltpu.make_async_copy(adj_hbm.at[0, 0], tiles, tile_sem)
     tile_load.start()
 
-    loads[0].wait()
-    for c in range(CHUNKS):
+    def transpose(c):
         eye = (
             lax.broadcasted_iota(I32, (SIZES[c], FEAT), 0) + STARTS[c]
             == lax.broadcasted_iota(I32, (SIZES[c], FEAT), 1)
@@ -138,6 +137,12 @@
         for b in range(DEST):
             held[c][k, j, b] = nt(eye, x_ref[b * BLK : (b + 1) * BLK, :]).astype(BF16)
 
+    loads[0].wait()
+    started = ORDER[0][1]
+    transpose(started)
+    for c in range(CHUNKS):
+        sums[c][SLOTS] = jnp.zeros((SIZES[c], BLK), F32)
+    degs[SLOTS] = jnp.zeros((8, BLK), F32)
     pl.semaphore_wait(barrier, len(peers))
 
     sent = []
@@ -168,6 +173,8 @@
         return held[c].at[k if kk is None else kk, jj, pl.ds(lo, n)]
 
     def own_out(c):
+        if c != started:
+            transpose(c)
         mine = part(c, j, 0, 4)
         send(c, 0, mine, part(c, j, 12, 4), a_plus)
         send(c, 1, mine, part(c, j, 4, 4), a_minus)
@@ -422,9 +429,6 @@
                 acc[here, :] = total
 
     def prepare():
-        for c in range(CHUNKS):
-            sums[c][SLOTS] = jnp.zeros((SIZES[c], BLK), F32)
-        degs[SLOTS] = jnp.zeros((8, BLK), F32)
         make_plan()
         own_part()
 

time: 61.7 us -> 61.5 us (level)
  no operation moved by 1% of the time
where the time goes in v5:
time: 61.5 us; the launch traced here: 61.3 us
  Pallas kernels  59.9 us (97%)
  local copies, waits for them, and re-layouts  0.8 us (1%)
  between operations  0.66 us (1%)
    pallas_call x1, Pallas kernels, per_device(): pl.pallas_call(layer_kernel, out_shape=pltpu.VMEM((DEST * BLK, HID), BF16...  59.9 us

profile of v5, /device:TPU:1, one launch (start us, length us, event | category | flops | bytes accessed | tf_op | source)
XLA Modules:
  0.0 61.3 jit_solution(15588724613739427563)
XLA Ops:
  0.7 59.9 %shard_map.82 = bf16[1024,256]{1,0:T(8,128)(2,1)S(1)} custom-call(s32[1,1]{1,0:T(1,128)S(6)} %copy.11.counts, s32[1,1,64]{2,1,0:T(1,128)} %rows_ref.1, s32[1,1,64]{2,1,0:T(1,128)} %cols_ref.1, bf16[1024,128]{1,0:T(8,128)(2,1)} %x_hbm.1, bf16[1,1,64,256,256]{4,3,2,1,0:T(8,128)(2,1)} %adj_hbm.1, bf16[128,256]{1,0:T(8,128)(2,1)} %ws_hbm.1, ...), custom_call_target="tpu_custom_call" | custom-call | tf_op jit(solution)/shard_map/pallas_call | solution.py:478
  60.5 0.8 %copy.10 = bf16[1024,256]{1,0:T(8,128)(2,1)} copy(bf16[1024,256]{1,0:T(8,128)(2,1)S(1)} %shard_map.82) | data formatting | bytes 1048576
